TPU v7x, 256 devices: a whole 4x4x8 slice. The times are simulated.
256 devices in a mesh: seq: 32 (over y_hi, z, core), tp: 8 (over x, y_lo).
Axes of the slice: x: 4, y: 4 (y_hi: 2, y_lo: 2; y = y_hi * 2 + y_lo), z: 8, core: 2. Of those that a mesh axis runs over, the one named last changes fastest.
Arguments:
- hidden: bfloat16 [4096, 7168], P('seq', 'tp'), may hold values from -6 to 6
- w_kv_down: bfloat16 [7168, 576], P('tp'), may hold values from -0.0625 to 0.0625
- kv_gain: float32 [512], replicated, may hold values from 0.1 to 1.9
- q_latent: bfloat16 [4096, 64, 512], P('seq', 'tp'), may hold values from -300 to 300
- q_rope: bfloat16 [4096, 4096], P('seq', 'tp'), may hold values from -6 to 6
- w_value: bfloat16 [64, 512, 128], P('tp'), may hold values from -0.75 to 0.75
Outputs:
- attended: bfloat16 [4096, 8192], P('seq', 'tp')
All inputs are finite; a program needn't handle non-finite values.
Results may differ from a plain program's by a relative error of at most 0.0097.
Values may be sent and summed in bfloat16 or wider, within the bound.
A program may use at most 64 MiB of HBM per device.

v0:
```python
import jax
import jax.numpy as jnp
from jax import lax
from jax.sharding import PartitionSpec as P

KV_RANK = 512
ROPE = 64


SCORE_SCALE = 192.0 ** (-0.5)
ROPE_BASE = 10000.0
EPSILON = 1e-06


def from_everyone(shard, axis):
    size = lax.axis_size(axis)
    return lax.all_to_all(
        jnp.broadcast_to(shard[None], (size, *shard.shape)), axis, 0, 0, tiled=True
    )


def of_everyone(shard, axis):
    everything = from_everyone(shard, axis)
    return jnp.sum(everything, axis=0)


def rotate(values, positions):
    full_width = values.shape[-1]
    half_width = full_width // 2
    frequency = ROPE_BASE ** (-jnp.arange(half_width, dtype=jnp.float32) * 2.0 / full_width)
    angles = positions.astype(jnp.float32)[:, None] * frequency[None, :]
    angle_shape = (angles.shape[0],) + (1,) * (values.ndim - 2) + (half_width,)
    cosine = jnp.cos(angles).reshape(angle_shape)
    sine_part = jnp.sin(angles).reshape(angle_shape)
    first_half = values[..., :half_width]
    second_half = values[..., half_width:]
    return jnp.concatenate(
        [
            first_half * cosine - second_half * sine_part,
            first_half * sine_part + second_half * cosine,
        ],
        -1,
    )


def finish(projection, kv_gain, positions):
    latent_part = projection[:, :KV_RANK]
    mean_square = jnp.mean(latent_part * latent_part, axis=-1, keepdims=True)
    normed = latent_part * lax.rsqrt(mean_square + EPSILON) * kv_gain[None, :]
    rope_part = rotate(projection[:, KV_RANK:], positions)
    return jnp.concatenate([normed, rope_part], -1).astype(jnp.bfloat16)


def update(running, group_queries, group_start, key_piece, key_start):
    query_count = group_queries.shape[0]
    key_count = key_piece.shape[0]

    def attend(current):
        top_score, weight_total, weighted = current
        scores = (
            jnp.einsum("qhc,kc->hqk", group_queries, key_piece, preferred_element_type=jnp.float32)
            * SCORE_SCALE
        )
        key_positions = jnp.arange(key_count, dtype=jnp.int32)
        query_positions = group_start + jnp.arange(query_count, dtype=jnp.int32)
        allowed = (key_positions[None, :] <= query_positions[:, None])[None]
        scores = jnp.where(allowed, scores, -1e30)
        new_max = jnp.maximum(top_score, jnp.max(scores, axis=-1))
        rescale = jnp.exp(top_score - new_max)
        weights = jnp.where(allowed, jnp.exp(scores - new_max[..., None]), 0.0)
        new_total = jnp.sum(weights, axis=-1)
        added_term = jnp.einsum(
            "hqk,kc->hqc",
            weights.astype(jnp.bfloat16),
            key_piece[:, :KV_RANK],
            preferred_element_type=jnp.float32,
        )
        return (new_max, new_total, added_term)

    return lax.cond(
        key_start <= group_start + query_count - 1, attend, lambda unchanged: unchanged, running
    )


def project(running, w_value):
    latent_out = (running[2] / running[1][..., None]).astype(jnp.bfloat16)
    projected = jnp.einsum("hqc,hcv->qhv", latent_out, w_value, preferred_element_type=jnp.float32)
    return projected.astype(jnp.bfloat16).reshape(projected.shape[0], -1)


def shards(hidden, w_kv_down, kv_gain, q_latent, q_rope, w_value):
    tok_rows = hidden.shape[0]
    heads_here = q_latent.shape[1]
    seq_index = lax.axis_index("seq")
    own_start = seq_index * tok_rows
    partial_value = jnp.dot(hidden, w_kv_down, preferred_element_type=jnp.float32)
    summed = of_everyone(partial_value, "tp")
    key_here = finish(summed, kv_gain, own_start + jnp.arange(tok_rows, dtype=jnp.int32))
    rope_query = rotate(
        q_rope.astype(jnp.float32).reshape(tok_rows, heads_here, ROPE),
        own_start + jnp.arange(tok_rows, dtype=jnp.int32),
    ).astype(jnp.bfloat16)
    queries = jnp.concatenate([q_latent, rope_query], -1)
    query_groups = ((queries, own_start),)

    def fresh_state(query_count):
        return (
            jnp.full((heads_here, query_count), -1e30, jnp.float32),
            jnp.zeros((heads_here, query_count), jnp.float32),
            jnp.zeros((heads_here, query_count, KV_RANK), jnp.float32),
        )

    fold_states = tuple((fresh_state(group[0].shape[0]) for group in query_groups))

    def absorb(running_all, key_piece, key_start):
        return tuple(
            (
                update(running, group[0], group[1], key_piece, key_start)
                for running, group in zip(running_all, query_groups)
            )
        )

    fold_states = absorb(
        fold_states, lax.all_gather(key_here, "seq", axis=0, tiled=True), jnp.int32(0)
    )
    results = [project(running, w_value) for running in fold_states]
    return results[0]


def solution(mesh):
    placed = (
        P("seq", "tp"),
        P("tp", None),
        P(),
        P("seq", "tp", None),
        P("seq", "tp"),
        P("tp", None, None),
    )
    return jax.shard_map(
        shards, mesh=mesh, in_specs=placed, out_specs=P("seq", "tp"), check_vma=False
    )
```

profile of v0, /device:TPU:27, one launch (start us, length us, event | category | flops | bytes accessed | tf_op | source)
XLA Modules:
  0.0 185.5 jit_solution(8439557678805121426)
XLA Ops:
  6.5 0.0 copy-start
  6.5 1.8 fusion.11
  8.4 0.0 copy-start.2
  8.4 1.6 broadcast_in_dim.44
  10.0 0.0 copy-start.1
  10.0 5.3 %all-to-all-start = ((f32[8,128,576]{1,2,0:T(8,128)}), f32[8,128,576]{1,2,0:T(8,128)S(1)}, u32[]{:S(2)}, u32[]{:S(2)}) async-start(f32[8,128,576]{1,2,0:T(8,128)} %broadcast_in_dim.44), calls=%async_computation | async-start | bytes 4718592 | tf_op jit(solution)/shard_map/all_to_all | solution.py:17
  15.3 0.0 all-gather.2.cloned.1.call-start
  15.3 30.3 %all-to-all-done = f32[8,128,576]{1,2,0:T(8,128)S(1)} async-done(((f32[8,128,576]{1,2,0:T(8,128)}), f32[8,128,576]{1,2,0:T(8,128)S(1)}, u32[]{:S(2)}, u32[]{:S(2)}) %all-to-all-start) | async-done | bytes 2359328 | tf_op jit(solution)/shard_map/all_to_all | solution.py:17
  45.6 0.8 reduce_sum.27
  46.4 1.0 multiply_reduce_fusion
  47.5 0.9 multiply_cosine_fusion
  48.4 0.0 copy-done.2
  48.4 1.1 multiply_convert_fusion
  49.5 0.7 pad_maximum_fusion.1
  50.1 0.0 all-gather.2.cloned.1.call-update
  50.2 0.0 copy-done.1
  50.2 0.1 copy.26
  50.3 1.9 %copy.27 = bf16[128,8,512]{0,2,1:T(8,128)(2,1)S(1)} copy(bf16[128,8,512]{2,1,0:T(8,128)(2,1)} %param.11) | data formatting | bytes 2097152 | tf_op args[3]
  52.3 1.1 pad_maximum_fusion
  53.4 90.0 %all-gather.2.cloned.1.call-done = bf16[4096,576]{0,1:T(8,128)(2,1)} async-done(((bf16[128,576]{0,1:T(8,128)(2,1)}), bf16[4096,576]{0,1:T(8,128)(2,1)}) %all-gather.2.cloned.1.call-update) | async-done | bytes 4718608 | tf_op jit(solution)/shard_map/all_gather | solution.py:124
  143.4 32.2 %conditional.1 = (f32[8,128]{1,0:T(8,128)S(1)}, f32[8,128,512]{2,1,0:T(8,128)}) conditional(s32[]{:T(128)} %convert_element_type.26, () %tuple.13, (s32[]{:T(128)}, bf16[4096,576]{0,1:T(8,128)(2,1)}, bf16[128,8,576]{0,2,1:T(8,128)(2,1)}) %tuple.14), branch_computations={%region_2.0_spmd, %region_3.6_spmd} | conditional | flops 9181854720 | bytes 74081296 | solution.py:80
  143.4 1.2 iota_compare_fusion
  144.6 7.6 %copy.28 = bf16[4096,576]{1,0:T(8,128)(2,1)} copy(bf16[4096,576]{0,1:T(8,128)(2,1)} %get-tuple-element.19) | data formatting | bytes 9437184 | tf_op jit(solution)/shard_map
  152.2 10.0 %fusion = (f32[8,128]{1,0:T(8,128)S(1)}, f32[4096,128,8]{1,0,2:T(8,128)S(1)}) fusion(pred[128,4096]{0,1:T(8,128)(4,1)} %iota_compare_fusion, bf16[128,8,576]{0,2,1:T(8,128)(2,1)} %get-tuple-element.13, bf16[4096,576]{0,1:T(8,128)(2,1)} %get-tuple-element.19), kind=kOutput, calls=%fused_computation.2 | convolution fusion | flops 4844420096 | bytes 23203840 | tf_op jit(solution)/shard_map/cond/branch_1_fun/qhc,kc->hqk/dot_general | solution.py:61
  162.2 8.4 %fusion.3 = f32[8,128,512]{2,1,0:T(8,128)} fusion(f32[4096,128,8]{1,0,2:T(8,128)S(1)} %get-tuple-element.22, f32[8,128]{1,0:T(8,128)S(1)} %broadcast_maximum_fusion, pred[128,4096]{0,1:T(8,128)(4,1)} %iota_compare_fusion, bf16[4096,576]{1,0:T(8,128)(2,1)} %copy.28), kind=kOutput, calls=%fused_computation.5 | convolution fusion | flops 4315938816 | bytes 23597056 | tf_op jit(solution)/shard_map/cond/branch_1_fun/hqk,kc->hqc/dot_general | solution.py:72
  170.7 4.9 %fusion.2 = f32[8,128]{1,0:T(8,128)S(1)} fusion(f32[4096,128,8]{1,0,2:T(8,128)S(1)} %get-tuple-element.22, f32[8,128]{1,0:T(8,128)S(1)} %broadcast_maximum_fusion, pred[128,4096]{0,1:T(8,128)(4,1)} %iota_compare_fusion), kind=kLoop, calls=%fused_computation.4 | loop fusion | flops 20970496 | bytes 17309696 | tf_op jit(solution)/shard_map/cond/branch_1_fun/reduce_sum | solution.py:71
  175.6 0.0 copy-done
  175.6 2.2 %convolution_convert_fusion = bf16[8,128,128]{1,2,0:T(8,128)(2,1)S(1)} fusion(bf16[8,512,128]{2,1,0:T(8,128)(2,1)S(1)} %copy-done, f32[8,128,512]{2,1,0:T(8,128)} %get-tuple-element.16, f32[8,128]{1,0:T(8,128)S(1)} %get-tuple-element.17), kind=kOutput, calls=%fused_computation.17 | convolution fusion | flops 135397376 | bytes 3411968 | tf_op jit(solution)/shard_map/hqc,hcv->qhv/dot_general | solution.py:87
  177.8 0.9 copy.30
  (6 shorter events, 0.1 us)
Async XLA Ops:
  6.5 169.1 %copy-start = (bf16[8,512,128]{2,1,0:T(8,128)(2,1)S(1)}, bf16[8,512,128]{2,1,0:T(8,128)(2,1)}, u32[]{:S(2)}) copy-start(bf16[8,512,128]{2,1,0:T(8,128)(2,1)} %param.13) | copy-start | bytes 3145732
  8.4 40.0 %copy-start.2 = (f32[512]{0:T(512)S(1)}, f32[512]{0:T(512)}, u32[]{:S(2)}) copy-start(f32[512]{0:T(512)} %param.10) | copy-start | bytes 6148
  10.0 40.2 %copy-start.1 = (bf16[128,512]{1,0:T(8,128)(2,1)S(1)}, bf16[128,512]{1,0:T(8,128)(2,1)}, u32[]{:S(2)}) copy-start(bf16[128,512]{1,0:T(8,128)(2,1)} %param.12) | copy-start | bytes 393220
  10.0 35.6 %all-to-all-start = ((f32[8,128,576]{1,2,0:T(8,128)}), f32[8,128,576]{1,2,0:T(8,128)S(1)}, u32[]{:S(2)}, u32[]{:S(2)}) async-start(f32[8,128,576]{1,2,0:T(8,128)} %broadcast_in_dim.44), calls=%async_computation | async-start | bytes 4718592 | tf_op jit(solution)/shard_map/all_to_all | solution.py:17
  15.3 128.1 %all-gather.2.cloned.1.call-start = ((), (), s32[]{:S(2)}) async-start(), calls=%async_computation.1 | async-start | bytes 4866048 | tf_op jit(solution)/shard_map/all_gather | solution.py:124
Sparse Core Ops, SparseCore 0:
  50.3 93.1 all-gather.1
where the time goes:
time: 189 us; the launch traced here: 186 us
  waiting for transfers between devices  120 us (63%)
  matrix products  22.5 us (12%)
  between operations  13.5 us (7%)
  local copies, waits for them, and re-layouts  12.1 us (6%)
  other arithmetic  11.8 us (6%)
  starting transfers between devices  5.3 us (3%)
    all_gather x1, waiting for transfers between devices, shards(): lax.all_gather(key_here, 'seq', axis=0, tiled=True)  90 us
    all_to_all x1, waiting for transfers between devices, from_everyone(): lax.all_to_all(jnp.broadcast_to(shard[None], (size, *shard.shape)), axis,...  30.3 us
    dot_general x1, matrix products, attend(): jnp.einsum('qhc,kc->hqk', group_queries, key_piece, preferred_element_typ...  9.97 us
    dot_general x1, matrix products, attend(): jnp.einsum('hqk,kc->hqc', weights.astype(jnp.bfloat16), key_piece[:, :KV_...  8.44 us
    another operation x1, local copies, waits for them, and re-layouts  7.63 us
    all_to_all x1, starting transfers between devices, from_everyone(): lax.all_to_all(jnp.broadcast_to(shard[None], (size, *shard.shape)), axis,...  5.3 us
    reduce_sum x1, other arithmetic, attend(): new_total = jnp.sum(weights, axis=-1)  4.93 us
  transfers between devices with their start and end apart: 2, of which 2 were waited for; matrix products, arithmetic and copies ran while one was open for 2% of the time, Pallas kernels for 0%

commit v1 on v0

v1 whole, which is shorter than its diff:
```python
import jax
import jax.numpy as jnp
import numpy as np
from jax import lax
from jax.experimental import pallas as pl
from jax.experimental.pallas import tpu as pltpu
from jax.sharding import PartitionSpec as P

MESH = pl.DeviceIdType.MESH
KV_RANK = 512
ROPE = 64
WIDTH = KV_RANK + ROPE
V_DIM = 128
TOK = 128
HEADS = 8
ROWS = TOK * HEADS
TP = 8
SLICE = TOK // TP
UNIT = 8 * SLICE
BLOCK = 4 * UNIT
EPSILON = 1e-06
LOG2E = 1.4426950408889634
EXP_SCALE = 192.0 ** (-0.5) * LOG2E
NT = (((1,), (1,)), ((), ()))
NN = (((1,), (0,)), ((), ()))
TN = (((0,), (0,)), ((), ()))


def dot(a, b, dims):
    return lax.dot_general(a, b, dims, preferred_element_type=jnp.float32)


def kernel(
    hidden, w_down, gain, q_latent, q_rope, w_value, freq, out,
    hid_v, wd_v, ql_v, qr_v, wv_v, partial, sums, keys, q_f32, queries, cos_t, sin_t, acc, top, total,
    load_sem, rs_s, rs_r, z_s, z_r, a_s, a_r, b_s, b_r, f_s, f_r, c_s, c_r,
):
    seq = lax.axis_index("seq")
    tp = lax.axis_index("tp")
    core = seq % 2
    z = (seq // 2) % 8
    y_hi = seq // 16
    x = tp // 2
    y_lo = tp % 2
    y = y_hi * 2 + y_lo

    def device(x_, y_, z_):
        return (((y_ // 2) * 8 + z_) * 2 + core, x_ * 2 + y_ % 2)

    a_me = x * (1 - core) + y * core
    b_me = y * (1 - core) + x * core

    def plane(a_, b_):
        return device(a_ * (1 - core) + b_ * core, b_ * (1 - core) + a_ * core, z)

    sibling = (seq + 1 - 2 * core, tp)

    loads = [
        pltpu.make_async_copy(src, dst, load_sem.at[i])
        for i, (src, dst) in enumerate(
            ((hidden, hid_v), (w_down, wd_v), (q_rope, qr_v), (q_latent, ql_v), (w_value, wv_v))
        )
    ]
    for load in loads:
        load.start()

    barrier = pltpu.get_barrier_semaphore()
    peers = [(seq, (tp + d) % TP) for d in range(1, TP)]
    peers += [device(x, y, (z + d) % 8) for d in range(1, 8)]
    peers += [sibling, device(x, 3 - y, z), device(x, (y + 2) % 4, z)]
    for peer in peers:
        pl.semaphore_signal(barrier, inc=1, device_id=peer, device_id_type=MESH)

    loads[0].wait()
    loads[1].wait()
    partial[...] = dot(hid_v[...], wd_v[...], NN)
    pl.semaphore_wait(barrier, len(peers))

    sent = []

    def copy(src, dst, send_sem, recv_sem, target):
        return pltpu.make_async_remote_copy(
            src_ref=src, dst_ref=dst, send_sem=send_sem, recv_sem=recv_sem, device_id=target, device_id_type=MESH
        )

    def start(*args):
        one = copy(*args)
        one.start()
        sent.append(one)

    def rows_of(owner):
        return partial.at[pl.ds(pl.multiple_of(owner * SLICE, SLICE), SLICE), :]

    for d in range(1, TP):
        owner = (tp + d) % TP
        start(rows_of(owner), sums.at[d], rs_s.at[d], rs_r.at[d], (seq, owner))

    positions = (seq * TOK + lax.broadcasted_iota(jnp.int32, (TOK, 128), 0)).astype(jnp.float32)
    angles = positions * freq[...]
    lane = lax.broadcasted_iota(jnp.int32, (1, 128), 1)
    cos_t[...] = jnp.cos(angles)
    sin_t[...] = jnp.where(lane % ROPE < ROPE // 2, -jnp.sin(angles), jnp.sin(angles))
    loads[2].wait()
    raw = qr_v[...].astype(jnp.float32)
    wide_lane = lax.broadcasted_iota(jnp.int32, (1, HEADS * ROPE), 1)
    swapped = jnp.where(
        wide_lane % ROPE < ROPE // 2,
        pltpu.roll(raw, HEADS * ROPE - ROPE // 2, 1),
        pltpu.roll(raw, ROPE // 2, 1),
    )
    repeat = HEADS * ROPE // 128
    rotated = raw * jnp.concatenate([cos_t[...]] * repeat, 1) + swapped * jnp.concatenate([sin_t[...]] * repeat, 1)
    rotated = rotated.astype(jnp.bfloat16)
    loads[3].wait()
    for c in range(KV_RANK // 128):
        q_f32[c] = ql_v[:, c * 128:(c + 1) * 128].astype(jnp.float32)
    for h in range(HEADS):
        for c in range(KV_RANK // 128):
            queries[h * TOK:(h + 1) * TOK, c * 128:(c + 1) * 128] = q_f32[
                c, pl.ds(h, TOK, stride=HEADS), :
            ].astype(jnp.bfloat16)
        queries[h * TOK:(h + 1) * TOK, KV_RANK:] = rotated[:, h * ROPE:(h + 1) * ROPE]

    for d in range(1, TP):
        copy(rows_of(tp), sums.at[d], rs_s.at[d], rs_r.at[d], (seq, tp)).wait_recv()
    mine = pl.ds(pl.multiple_of(tp * SLICE, SLICE), SLICE)
    projection = partial[mine, :]
    for d in range(1, TP):
        projection = projection + sums[d]
    latent = projection[:, :KV_RANK]
    mean_square = jnp.mean(latent * latent, axis=-1, keepdims=True)
    latent = latent * lax.rsqrt(mean_square + EPSILON) * gain[...]
    rope = projection[:, KV_RANK:]
    rope_swapped = jnp.concatenate([rope[:, ROPE // 2:], rope[:, :ROPE // 2]], 1)
    rope = rope * cos_t[mine, :ROPE] + rope_swapped * sin_t[mine, :ROPE]

    def unit(which, a_, b_):
        return keys.at[which, pl.ds(pl.multiple_of((b_ * 4 + a_) * UNIT, UNIT), UNIT), :]

    def slot(z_):
        return keys.at[core, pl.ds(pl.multiple_of(((b_me * 4 + a_me) * 8 + z_) * SLICE, SLICE), SLICE), :]

    slot(z)[...] = jnp.concatenate([latent, rope], 1).astype(jnp.bfloat16)

    for d in (4, 3, 5, 2, 6, 1, 7):
        start(slot(z), slot(z), z_s.at[d], z_r.at[d], device(x, y, (z + d) % 8))
    for d in range(1, 8):
        there = slot((z - d) % 8)
        copy(there, there, z_s.at[d], z_r.at[d], sibling).wait_recv()

    def to_sibling(i, a_, b_):
        here = unit(core, a_, b_)
        start(here, here, c_s.at[i], c_r.at[i], sibling)

    def to_b(i, a_):
        here = unit(core, a_, b_me)
        start(here, here, b_s.at[0, i], b_r.at[0, i], plane(a_me, (b_me + 1) % 4))
        start(here, here, b_s.at[1, i], b_r.at[1, i], plane(a_me, (b_me + 3) % 4))

    order = (0, 1, 3, 2)
    own = unit(core, a_me, b_me)
    for d in (2, 1, 3):
        start(own, own, a_s.at[d], a_r.at[d], plane((a_me + d) % 4, b_me))
    to_b(0, a_me)
    to_sibling(0, a_me, b_me)
    for i, d in enumerate(order[1:], 1):
        a_ = (a_me + 4 - d) % 4
        there = unit(core, a_, b_me)
        copy(there, there, a_s.at[d], a_r.at[d], sibling).wait_recv()
        to_b(i, a_)
        to_sibling(i, a_, b_me)

    def from_sibling(group, b_there):
        for i, d in enumerate(order):
            there = unit(1 - core, (b_me + 4 - d) % 4, b_there)
            copy(there, there, c_s.at[group * 4 + i], c_r.at[group * 4 + i], sibling).wait_recv()

    query_pos = seq * TOK + lax.broadcasted_iota(jnp.int32, (1, TOK), 1)

    def block_scores(which, b_):
        index = lax.broadcasted_iota(jnp.int32, (BLOCK, TOK), 0)
        a_i = index // UNIT
        z_i = (index // SLICE) % 8
        x_i = a_i * (1 - which) + b_ * which
        y_i = b_ * (1 - which) + a_i * which
        key_pos = (((y_i // 2) * 8 + z_i) * 2 + which) * TOK + (x_i * 2 + y_i % 2) * SLICE + index % SLICE
        bias = jnp.where(key_pos <= query_pos, 0.0, -1e30)
        rows = keys[which, pl.ds(pl.multiple_of(b_ * BLOCK, BLOCK), BLOCK), :]
        scores = dot(rows, queries[...], NT) + jnp.concatenate([bias] * HEADS, 1)
        return rows, scores

    def attend(b_own, b_other, first):
        rows_0, scores_0 = block_scores(core, b_own)
        rows_1, scores_1 = block_scores(1 - core, b_other)
        here = jnp.maximum(jnp.max(scores_0, 0, keepdims=True), jnp.max(scores_1, 0, keepdims=True))
        new_top = here if first else jnp.maximum(top[0:1, :], here)
        shift = new_top * EXP_SCALE
        weights_0 = jnp.exp2(scores_0 * EXP_SCALE - shift)
        weights_1 = jnp.exp2(scores_1 * EXP_SCALE - shift)
        added = jnp.sum(weights_0, 0, keepdims=True) + jnp.sum(weights_1, 0, keepdims=True)
        mixed = dot(rows_0[:, :KV_RANK], weights_0.astype(jnp.bfloat16), TN) + dot(
            rows_1[:, :KV_RANK], weights_1.astype(jnp.bfloat16), TN
        )
        if first:
            total[0:1, :] = added
            acc[...] = mixed
        else:
            scale = jnp.exp2(top[0:1, :] * EXP_SCALE - shift)
            total[0:1, :] = total[0:1, :] * scale + added
            acc[...] = acc[...] * scale + mixed
        top[0:1, :] = new_top

    b_less, b_more, b_far = (b_me + 3) % 4, (b_me + 1) % 4, (b_me + 2) % 4
    a_less, a_more, a_far = (a_me + 3) % 4, (a_me + 1) % 4, (a_me + 2) % 4

    from_sibling(0, a_me)
    attend(b_me, a_me, True)

    for i, d in enumerate(order):
        a_ = (a_me + 4 - d) % 4
        there = unit(core, a_, b_less)
        copy(there, there, b_s.at[0, i], b_r.at[0, i], sibling).wait_recv()
        if i < 2:
            start(there, there, f_s.at[i], f_r.at[i], plane(a_me, b_more))
        to_sibling(4 + i, a_, b_less)
    for i, d in enumerate(order):
        a_ = (a_me + 4 - d) % 4
        there = unit(core, a_, b_more)
        copy(there, there, b_s.at[1, i], b_r.at[1, i], sibling).wait_recv()
        if i >= 2:
            start(there, there, f_s.at[i], f_r.at[i], plane(a_me, b_less))
        to_sibling(8 + i, a_, b_more)

    from_sibling(1, a_less)
    attend(b_less, a_less, False)
    from_sibling(2, a_more)
    attend(b_more, a_more, False)
    for i, d in enumerate(order):
        a_ = (a_me + 4 - d) % 4
        there = unit(core, a_, b_far)
        copy(there, there, f_s.at[i], f_r.at[i], sibling).wait_recv()
        to_sibling(12 + i, a_, b_far)
    from_sibling(3, a_far)
    attend(b_far, a_far, False)

    loads[4].wait()
    mixed = (acc[...] / total[0:1, :]).astype(jnp.bfloat16)
    for h in range(HEADS):
        cut = slice(h * TOK, (h + 1) * TOK)
        out[:, h * V_DIM:(h + 1) * V_DIM] = dot(mixed[:, cut], wv_v[h], TN).astype(jnp.bfloat16)
    for one in sent:
        one.wait_send()


def shards(hidden, w_kv_down, kv_gain, q_latent, q_rope, w_value):
    half = ROPE // 2
    frequency = (10000.0 ** (-np.arange(half, dtype=np.float64) * 2.0 / ROPE)).astype(np.float32)
    freq = jnp.asarray(np.tile(frequency, 4)[None, :])
    hbm = pl.BlockSpec(memory_space=pl.ANY)
    vmem = pl.BlockSpec(memory_space=pltpu.VMEM)
    bf16, f32 = jnp.bfloat16, jnp.float32
    dma = pltpu.SemaphoreType.DMA
    width = hidden.shape[1]
    return pl.pallas_call(
        kernel,
        name="latent_attention",
        out_shape=jax.ShapeDtypeStruct((TOK, HEADS * V_DIM), bf16),
        in_specs=[hbm, hbm, vmem, hbm, hbm, hbm, vmem],
        out_specs=vmem,
        scratch_shapes=[
            pltpu.VMEM((TOK, width), bf16),
            pltpu.VMEM((width, WIDTH), bf16),
            pltpu.VMEM((ROWS, KV_RANK), bf16),
            pltpu.VMEM((TOK, HEADS * ROPE), bf16),
            pltpu.VMEM((HEADS, KV_RANK, V_DIM), bf16),
            pltpu.VMEM((TOK, WIDTH), f32),
            pltpu.VMEM((TP, SLICE, WIDTH), f32),
            pltpu.VMEM((2, 4 * BLOCK, WIDTH), bf16),
            pltpu.VMEM((KV_RANK // 128, ROWS, 128), f32),
            pltpu.VMEM((ROWS, WIDTH), bf16),
            pltpu.VMEM((TOK, 128), f32),
            pltpu.VMEM((TOK, 128), f32),
            pltpu.VMEM((KV_RANK, ROWS), f32),
            pltpu.VMEM((8, ROWS), f32),
            pltpu.VMEM((8, ROWS), f32),
            dma((5,)),
            dma((8,)), dma((8,)),
            dma((8,)), dma((8,)),
            dma((4,)), dma((4,)),
            dma((2, 4)), dma((2, 4)),
            dma((4,)), dma((4,)),
            dma((16,)), dma((16,)),
        ],
        compiler_params=pltpu.CompilerParams(
            collective_id=0, has_side_effects=True, vmem_limit_bytes=50 * 2**20
        ),
    )(
        hidden,
        w_kv_down,
        kv_gain[None, :],
        q_latent.reshape(ROWS, KV_RANK),
        q_rope,
        w_value,
        freq,
    )


def solution(mesh):
    placed = (
        P("seq", "tp"),
        P("tp", None),
        P(),
        P("seq", "tp", None),
        P("seq", "tp"),
        P("tp", None, None),
    )
    return jax.shard_map(
        shards, mesh=mesh, in_specs=placed, out_specs=P("seq", "tp"), check_vma=False
    )
```

time: 189 us -> 58 us (0.31)
  the two profiles are of different devices: /device:TPU:27 before, /device:TPU:1 now
where the time goes in v1:
time: 58 us; the launch traced here: 57.9 us
  Pallas kernels  53.1 us (92%)
  local copies, waits for them, and re-layouts  4.74 us (8%)
    pallas_call x1, Pallas kernels, shards(): pl.pallas_call(kernel, name='latent_attention', out_shape=jax.ShapeDtypeS...  53.1 us
    unnamed x14, local copies, waits for them, and re-layouts  4.74 us

profile of v1, /device:TPU:1, one launch (start us, length us, event | category | flops | bytes accessed | tf_op | source)
XLA Modules:
  0.0 57.9 jit_solution(12629582989458183034)
XLA Ops:
  0.0 0.0 copy-start.5
  0.0 0.0 copy-start.1
  0.0 0.0 copy-start
  0.0 0.0 copy-start.4
  0.0 2.2 %copy.8.w_down = bf16[896,576]{1,0:T(8,128)(2,1)S(1)} copy(bf16[896,576]{0,1:T(8,128)(2,1)} %param.8) | data formatting | bytes 2064384 | tf_op args[1]
  2.2 0.0 copy-done.5
  2.2 0.0 copy-done.1
  2.2 0.0 copy-done
  2.2 0.0 copy-done.4
  2.2 0.0 copy-start.2
  2.3 0.9 %copy-done.2 = bf16[128,896]{1,0:T(8,128)(2,1)S(1)} copy-done((bf16[128,896]{1,0:T(8,128)(2,1)S(1)}, bf16[128,896]{1,0:T(8,128)(2,1)}, u32[]{:S(2)}) %copy-start.2) | copy-done | bytes 229400
  3.2 0.0 copy-start.3
  3.2 0.9 %copy-done.3 = bf16[128,512]{1,0:T(8,128)(2,1)S(1)} copy-done((bf16[128,512]{1,0:T(8,128)(2,1)S(1)}, bf16[128,512]{1,0:T(8,128)(2,1)}, u32[]{:S(2)}) %copy-start.3) | copy-done | bytes 131096
  4.1 53.1 %latent_attention.1 = bf16[128,1024]{1,0:T(8,128)(2,1)S(1)} custom-call(bf16[128,896]{1,0:T(8,128)(2,1)S(1)} %copy-done.2, bf16[896,576]{1,0:T(8,128)(2,1)S(1)} %copy.8.w_down, f32[1,512]{1,0:T(1,128)S(1)} %bitcast.3, bf16[1024,512]{1,0:T(8,128)(2,1)S(1)} %bitcast.2, bf16[128,512]{1,0:T(8,128)(2,1)S(1)} %copy-done.3, bf16[8,512,128]{2,1,0:T(8,128)(2,1)S(1)} %copy-done.1, ...), custom_call_target="tpu_custom_call" | custom-call | tf_op jit(solution)/shard_map/latent_attention/pallas_call | solution.py:264
  57.2 0.7 %copy.10 = bf16[128,1024]{1,0:T(8,128)(2,1)} copy(bf16[128,1024]{1,0:T(8,128)(2,1)S(1)} %latent_attention.1) | data formatting | bytes 524288
Async XLA Ops:
  0.0 2.2 %copy-start.5 = (f32[1,128]{1,0:T(1,128)S(1)}, f32[1,128]{1,0:T(1,128)}, u32[]{:S(2)}) copy-start(f32[1,128]{1,0:T(1,128)} %constant.2.clone.freq) | copy-start | bytes 1540
  0.0 2.2 %copy-start.1 = (bf16[8,512,128]{2,1,0:T(8,128)(2,1)S(1)}, bf16[8,512,128]{2,1,0:T(8,128)(2,1)}, u32[]{:S(2)}) copy-start(bf16[8,512,128]{2,1,0:T(8,128)(2,1)} %w_value.1) | copy-start | bytes 3145732
  0.0 2.2 %copy-start = (bf16[128,8,512]{2,1,0:T(8,128)(2,1)S(1)}, bf16[128,8,512]{2,1,0:T(8,128)(2,1)}, u32[]{:S(2)}) copy-start(bf16[128,8,512]{2,1,0:T(8,128)(2,1)} %param.10) | copy-start | bytes 3145732
  0.0 2.2 %copy-start.4 = (f32[512]{0:T(512)S(1)}, f32[512]{0:T(512)}, u32[]{:S(2)}) copy-start(f32[512]{0:T(512)} %param.9) | copy-start | bytes 6148
  2.2 0.9 %copy-start.2 = (bf16[128,896]{1,0:T(8,128)(2,1)S(1)}, bf16[128,896]{1,0:T(8,128)(2,1)}, u32[]{:S(2)}) copy-start(bf16[128,896]{1,0:T(8,128)(2,1)} %hidden.1) | copy-start | bytes 688132
  3.2 0.9 %copy-start.3 = (bf16[128,512]{1,0:T(8,128)(2,1)S(1)}, bf16[128,512]{1,0:T(8,128)(2,1)}, u32[]{:S(2)}) copy-start(bf16[128,512]{1,0:T(8,128)(2,1)} %q_rope.1) | copy-start | bytes 393220

commit v2 on v1

v2 whole, which is shorter than its diff:
```python
import functools

import jax
import jax.numpy as jnp
import numpy as np
from jax import lax
from jax.experimental import pallas as pl
from jax.experimental.pallas import tpu as pltpu
from jax.sharding import PartitionSpec as P

MESH = pl.DeviceIdType.MESH
KV_RANK = 512
ROPE = 64
WIDTH = KV_RANK + ROPE
V_DIM = 128
TOK = 128
HEADS = 8
ROWS = TOK * HEADS
TP = 8
SLICE = TOK // TP
UNIT = 8 * SLICE
EPSILON = 1e-06
LOG2E = 1.4426950408889634
EXP_SCALE = 192.0 ** (-0.5) * LOG2E
NT = (((1,), (1,)), ((), ()))
TN = (((0,), (0,)), ((), ()))


def dot(a, b, dims):
    return lax.dot_general(a, b, dims, preferred_element_type=jnp.float32)


def maybe(cond, act):
    if cond is True:
        act()
    else:
        pl.when(cond)(act)


ME, MATE, CROSS, FAR = range(4)
NEAR = (ME, MATE)


def near(i, label):
    sign = 1 - 2 * (i % 2)
    return (i + (0, sign, 4 - sign, 2)[label]) % 4


def arrange():
    stages = (
        ((ME, ME),),
        ((MATE, ME), (CROSS, ME), (FAR, ME), (ME, MATE), (ME, CROSS)),
        ((CROSS, MATE), (FAR, MATE), (MATE, CROSS), (CROSS, CROSS)),
        ((MATE, MATE), (FAR, CROSS)),
        ((ME, FAR), (CROSS, FAR)),
        ((MATE, FAR), (FAR, FAR)),
    )
    labels = []
    for masked in (True, False):
        for stage in stages:
            for lineage in range(2):
                labels += [(lineage, a, b) for a, b in stage if ((b, a)[lineage] in NEAR) == masked]
    return labels


LABELS = arrange()
PLACE = {label: place for place, label in enumerate(LABELS)}


def kernel(
    hidden, w_down, gain, q_latent, q_rope, w_value, freq, out,
    hid_v, wd_v, ql_v, qr_v, wv_v, partial, sums, keys, q_f32, queries, cos_t, sin_t, acc, top, total,
    load_sem, rs_s, rs_r, z_s, z_r, a_s, a_r, b_s, b_r, f_s, f_r, c_s, c_r,
):
    seq = lax.axis_index("seq")
    tp = lax.axis_index("tp")
    core = seq % 2
    z = (seq // 2) % 8
    y_hi = seq // 16
    x = tp // 2
    y_lo = tp % 2
    y = y_hi * 2 + y_lo

    def device(x_, y_, z_):
        return (((y_ // 2) * 8 + z_) * 2 + core, x_ * 2 + y_ % 2)

    a_me = x * (1 - core) + y * core
    b_me = y * (1 - core) + x * core

    def plane(a_, b_):
        return device(a_ * (1 - core) + b_ * core, b_ * (1 - core) + a_ * core, z)

    sibling = (seq + 1 - 2 * core, tp)

    loads = [
        pltpu.make_async_copy(src, dst, load_sem.at[i])
        for i, (src, dst) in enumerate(
            ((hidden, hid_v), (w_down, wd_v), (q_rope, qr_v), (q_latent, ql_v), (w_value, wv_v))
        )
    ]
    for load in loads:
        load.start()

    barrier = pltpu.get_barrier_semaphore()
    peers = [(seq, (tp + d) % TP) for d in range(1, TP)]
    peers += [device(x, y, (z + d) % 8) for d in range(1, 8)]
    peers += [sibling, device(x, 3 - y, z), device(x, (y + 2) % 4, z)]
    for peer in peers:
        pl.semaphore_signal(barrier, inc=1, device_id=peer, device_id_type=MESH)

    loads[0].wait()
    loads[1].wait()
    partial[...] = dot(hid_v[...], wd_v[...], NT)
    pl.semaphore_wait(barrier, len(peers))

    sent = []

    def copy(src, dst, send_sem, recv_sem, target):
        return pltpu.make_async_remote_copy(
            src_ref=src, dst_ref=dst, send_sem=send_sem, recv_sem=recv_sem, device_id=target, device_id_type=MESH
        )

    def start(cond, *args):
        one = copy(*args)
        maybe(cond, one.start)
        sent.append((cond, one))

    def rows_of(owner):
        return partial.at[pl.ds(pl.multiple_of(owner * SLICE, SLICE), SLICE), :]

    for d in range(1, TP):
        owner = (tp + d) % TP
        start(True, rows_of(owner), sums.at[d], rs_s.at[d], rs_r.at[d], (seq, owner))

    positions = (seq * TOK + lax.broadcasted_iota(jnp.int32, (TOK, 128), 0)).astype(jnp.float32)
    angles = positions * freq[...]
    lane = lax.broadcasted_iota(jnp.int32, (1, 128), 1)
    cos_t[...] = jnp.cos(angles)
    sin_t[...] = jnp.where(lane % ROPE < ROPE // 2, -jnp.sin(angles), jnp.sin(angles))
    loads[2].wait()
    raw = qr_v[...].astype(jnp.float32)
    wide_lane = lax.broadcasted_iota(jnp.int32, (1, HEADS * ROPE), 1)
    swapped = jnp.where(
        wide_lane % ROPE < ROPE // 2,
        pltpu.roll(raw, HEADS * ROPE - ROPE // 2, 1),
        pltpu.roll(raw, ROPE // 2, 1),
    )
    repeat = HEADS * ROPE // 128
    rotated = raw * jnp.concatenate([cos_t[...]] * repeat, 1) + swapped * jnp.concatenate([sin_t[...]] * repeat, 1)
    rotated = rotated.astype(jnp.bfloat16)
    loads[3].wait()
    for c in range(KV_RANK // 128):
        q_f32[c] = ql_v[:, c * 128:(c + 1) * 128].astype(jnp.float32)
    for h in range(HEADS):
        for c in range(KV_RANK // 128):
            queries[h * TOK:(h + 1) * TOK, c * 128:(c + 1) * 128] = q_f32[
                c, pl.ds(h, TOK, stride=HEADS), :
            ].astype(jnp.bfloat16)
        queries[h * TOK:(h + 1) * TOK, KV_RANK:] = rotated[:, h * ROPE:(h + 1) * ROPE]

    for d in range(1, TP):
        copy(rows_of(tp), sums.at[d], rs_s.at[d], rs_r.at[d], (seq, tp)).wait_recv()
    mine = pl.ds(pl.multiple_of(tp * SLICE, SLICE), SLICE)
    projection = partial[mine, :]
    for d in range(1, TP):
        projection = projection + sums[d]
    latent = projection[:, :KV_RANK]
    mean_square = jnp.mean(latent * latent, axis=-1, keepdims=True)
    latent = latent * lax.rsqrt(mean_square + EPSILON) * gain[...]
    rope = projection[:, KV_RANK:]
    rope_swapped = jnp.concatenate([rope[:, ROPE // 2:], rope[:, :ROPE // 2]], 1)
    rope = rope * cos_t[mine, :ROPE] + rope_swapped * sin_t[mine, :ROPE]

    def unit_at(lineage, a, b):
        first, second = PLACE[0, a, b], PLACE[1, a, b]
        place = first + (second - first) * lineage
        return keys.at[pl.ds(pl.multiple_of(place * UNIT, UNIT), UNIT), :]

    def unit(a, b):
        return unit_at(core, a, b)

    own_place = PLACE[0, ME, ME] + (PLACE[1, ME, ME] - PLACE[0, ME, ME]) * core

    def slot(z_):
        return keys.at[pl.ds(pl.multiple_of(own_place * UNIT + z_ * SLICE, SLICE), SLICE), :]

    slot(z)[...] = jnp.concatenate([latent, rope], 1).astype(jnp.bfloat16)

    for d in (4, 3, 5, 2, 6, 1, 7):
        start(True, slot(z), slot(z), z_s.at[d], z_r.at[d], device(x, y, (z + d) % 8))
    for d in range(1, 8):
        there = slot((z - d) % 8)
        copy(there, there, z_s.at[d], z_r.at[d], sibling).wait_recv()

    early, late, even, odd = y_hi == 0, y_hi == 1, core == 0, core == 1

    def needed(lineage_even, a, b):
        if a in NEAR and b in NEAR:
            return True
        if b in NEAR:
            return late | lineage_even
        if a in NEAR:
            return late | jnp.logical_not(lineage_even)
        return late

    def send_a(a):
        cond = True if a == MATE else even | early
        start(cond, unit(ME, ME), unit(a, ME), a_s.at[a], a_r.at[a], plane(near(a_me, a), b_me))

    def send_b(a, b):
        if b == MATE:
            cond = True if a in NEAR else even | late
        else:
            cond = (even & early) | odd if a in NEAR else (even & early) | (odd & late)
        start(cond, unit(a, ME), unit(a, b), b_s.at[b, a], b_r.at[b, a], plane(a_me, near(b_me, b)))

    def forward(a):
        came, goes = (CROSS, MATE) if a in NEAR else (MATE, CROSS)
        if goes == MATE:
            cond = odd | late
        else:
            cond = (even & early) | (odd & late)
        start(cond, unit(a, came), unit(a, FAR), f_s.at[a], f_r.at[a], plane(a_me, near(b_me, goes)))

    def to_sibling(a, b):
        start(needed(even, a, b), unit(a, b), unit(a, b), c_s.at[b, a], c_r.at[b, a], sibling)

    def arrived(cond, ref, recv_sem):
        maybe(cond, copy(ref, ref, c_s.at[0, 0], recv_sem, sibling).wait_recv)

    def got_a(a):
        arrived(needed(even, a, ME), unit(a, ME), a_r.at[a])

    def got_b(a, b):
        arrived(needed(even, a, b), unit(a, b), b_r.at[b, a])

    def got_far(a):
        arrived(needed(even, a, FAR), unit(a, FAR), f_r.at[a])

    def got_sibling(*labels):
        for a, b in labels:
            arrived(needed(odd, a, b), unit_at(1 - core, a, b), c_r.at[b, a])

    row = lax.broadcasted_iota(jnp.int32, (UNIT, TOK), 0)
    token = lax.broadcasted_iota(jnp.int32, (UNIT, TOK), 1)
    ahead = (row // SLICE) * (2 * TOK) + row % SLICE - token

    def bias(place):
        lineage, a, b = LABELS[place]
        x_label, y_label = (a, b) if lineage == 0 else (b, a)
        base = (lineage - core - 2 * z) * TOK + (near(x, x_label) * 2 + near(y, y_label) % 2) * SLICE
        return jnp.concatenate([jnp.where(ahead + base <= 0, 0.0, -1e30)] * HEADS, 1)

    def attend(masked, free, first=False):
        rows, scores = [], []
        for (begin, end), is_masked in ((masked, True), (free, False)):
            if begin == end:
                continue
            rows.append(keys[begin * UNIT:end * UNIT, :])
            block = dot(rows[-1], queries[...], NT)
            if is_masked:
                block = block + jnp.concatenate([bias(place) for place in range(begin, end)], 0)
            scores.append(block)
        new_top = functools.reduce(jnp.maximum, [jnp.max(block, 0, keepdims=True) for block in scores])
        if not first:
            new_top = jnp.maximum(top[0:1, :], new_top)
        shift = new_top * EXP_SCALE
        added, mixed = 0.0, 0.0
        for keys_here, block in zip(rows, scores):
            weights = jnp.exp2(block * EXP_SCALE - shift)
            added = added + jnp.sum(weights, 0, keepdims=True)
            mixed = mixed + dot(keys_here[:, :KV_RANK], weights.astype(jnp.bfloat16), TN)
        if first:
            total[0:1, :] = added
            acc[...] = mixed
        else:
            scale = jnp.exp2(top[0:1, :] * EXP_SCALE - shift)
            total[0:1, :] = total[0:1, :] * scale + added
            acc[...] = acc[...] * scale + mixed
        top[0:1, :] = new_top

    def chunk(masked_late, free_late, masked_early):
        @pl.when(late)
        def _():
            attend(masked_late, free_late)

        if masked_early is not None:
            @pl.when(early)
            def _():
                attend(masked_early, (0, 0))

    for a in (MATE, CROSS, FAR):
        send_a(a)
    send_b(ME, MATE)
    send_b(ME, CROSS)
    to_sibling(ME, ME)
    got_sibling((ME, ME))
    attend((0, 2), (0, 0), first=True)

    got_a(MATE)
    send_b(MATE, CROSS)
    got_a(CROSS)
    send_b(CROSS, MATE)
    send_b(CROSS, CROSS)
    got_a(FAR)
    send_b(FAR, MATE)
    send_b(FAR, CROSS)
    send_b(MATE, MATE)
    for a in (MATE, CROSS, FAR):
        to_sibling(a, ME)
    got_b(ME, CROSS)
    forward(ME)
    to_sibling(ME, CROSS)
    got_b(ME, MATE)
    to_sibling(ME, MATE)
    got_sibling((MATE, ME), (CROSS, ME), (FAR, ME), (ME, CROSS), (ME, MATE))
    chunk((2, 9), (16, 19), (2, 9))

    got_b(CROSS, MATE)
    forward(CROSS)
    to_sibling(CROSS, MATE)
    got_b(MATE, CROSS)
    forward(MATE)
    to_sibling(MATE, CROSS)
    got_b(FAR, MATE)
    forward(FAR)
    to_sibling(FAR, MATE)
    got_b(CROSS, CROSS)
    to_sibling(CROSS, CROSS)
    got_sibling((CROSS, MATE), (MATE, CROSS), (FAR, MATE), (CROSS, CROSS))
    chunk((9, 12), (19, 24), None)

    got_b(MATE, MATE)
    to_sibling(MATE, MATE)
    got_b(FAR, CROSS)
    to_sibling(FAR, CROSS)
    got_sibling((MATE, MATE), (FAR, CROSS))

    @pl.when(early)
    def _():
        attend((9, 14), (0, 0))

    got_far(ME)
    to_sibling(ME, FAR)
    got_far(CROSS)
    to_sibling(CROSS, FAR)
    got_sibling((ME, FAR), (CROSS, FAR))
    chunk((12, 15), (24, 29), None)

    got_far(MATE)
    to_sibling(MATE, FAR)
    got_far(FAR)
    to_sibling(FAR, FAR)
    got_sibling((MATE, FAR), (FAR, FAR))
    chunk((15, 16), (29, 32), (14, 16))

    loads[4].wait()
    mixed = (acc[...] / total[0:1, :]).astype(jnp.bfloat16)
    for h in range(HEADS):
        cut = slice(h * TOK, (h + 1) * TOK)
        out[:, h * V_DIM:(h + 1) * V_DIM] = dot(mixed[:, cut], wv_v[h], TN).astype(jnp.bfloat16)
    for cond, one in sent:
        maybe(cond, one.wait_send)


def shards(hidden, w_kv_down, kv_gain, q_latent, q_rope, w_value):
    half = ROPE // 2
    frequency = (10000.0 ** (-np.arange(half, dtype=np.float64) * 2.0 / ROPE)).astype(np.float32)
    freq = jnp.asarray(np.tile(frequency, 4)[None, :])
    hbm = pl.BlockSpec(memory_space=pl.ANY)
    vmem = pl.BlockSpec(memory_space=pltpu.VMEM)
    bf16, f32 = jnp.bfloat16, jnp.float32
    dma = pltpu.SemaphoreType.DMA
    width = hidden.shape[1]
    return pl.pallas_call(
        kernel,
        name="latent_attention",
        out_shape=jax.ShapeDtypeStruct((TOK, HEADS * V_DIM), bf16),
        in_specs=[hbm, hbm, vmem, hbm, hbm, hbm, vmem],
        out_specs=vmem,
        scratch_shapes=[
            pltpu.VMEM((TOK, width), bf16),
            pltpu.VMEM((WIDTH, width), bf16),
            pltpu.VMEM((ROWS, KV_RANK), bf16),
            pltpu.VMEM((TOK, HEADS * ROPE), bf16),
            pltpu.VMEM((HEADS, KV_RANK, V_DIM), bf16),
            pltpu.VMEM((TOK, WIDTH), f32),
            pltpu.VMEM((TP, SLICE, WIDTH), f32),
            pltpu.VMEM((32 * UNIT, WIDTH), bf16),
            pltpu.VMEM((KV_RANK // 128, ROWS, 128), f32),
            pltpu.VMEM((ROWS, WIDTH), bf16),
            pltpu.VMEM((TOK, 128), f32),
            pltpu.VMEM((TOK, 128), f32),
            pltpu.VMEM((KV_RANK, ROWS), f32),
            pltpu.VMEM((8, ROWS), f32),
            pltpu.VMEM((8, ROWS), f32),
            dma((5,)),
            dma((8,)), dma((8,)),
            dma((8,)), dma((8,)),
            dma((4,)), dma((4,)),
            dma((4, 4)), dma((4, 4)),
            dma((4,)), dma((4,)),
            dma((4, 4)), dma((4, 4)),
        ],
        compiler_params=pltpu.CompilerParams(
            collective_id=0, has_side_effects=True, vmem_limit_bytes=60 * 2**20
        ),
    )(
        hidden,
        w_kv_down.T,
        kv_gain[None, :],
        q_latent.reshape(ROWS, KV_RANK),
        q_rope,
        w_value,
        freq,
    )


def solution(mesh):
    placed = (
        P("seq", "tp"),
        P("tp", None),
        P(),
        P("seq", "tp", None),
        P("seq", "tp"),
        P("tp", None, None),
    )
    return jax.shard_map(
        shards, mesh=mesh, in_specs=placed, out_specs=P("seq", "tp"), check_vma=False
    )
```

time: 58 us -> 55.4 us (0.955)
  the two profiles are of different devices: /device:TPU:1 before, /device:TPU:27 now
where the time goes in v2:
time: 55.4 us; the launch traced here: 55.2 us
  Pallas kernels  53.6 us (97%)
  local copies, waits for them, and re-layouts  1.67 us (3%)
    pallas_call x1, Pallas kernels, shards(): pl.pallas_call(kernel, name='latent_attention', out_shape=jax.ShapeDtypeS...  53.6 us
    unnamed x1, local copies, waits for them, and re-layouts  1.67 us

profile of v2, /device:TPU:27, one launch (start us, length us, event | category | flops | bytes accessed | tf_op | source)
XLA Modules:
  0.0 55.2 jit_solution(10504935862125121189)
XLA Ops:
  0.0 53.6 %latent_attention.1 = bf16[128,1024]{1,0:T(8,128)(2,1)} custom-call(bf16[128,896]{1,0:T(8,128)(2,1)} %hidden.1, bf16[576,896]{1,0:T(8,128)(2,1)} %bitcast.4, f32[1,512]{1,0:T(1,128)} %bitcast.5, bf16[1024,512]{1,0:T(8,128)(2,1)} %bitcast.3, bf16[128,512]{1,0:T(8,128)(2,1)} %q_rope.1, bf16[8,512,128]{2,1,0:T(8,128)(2,1)} %w_value.1, f32[1,128]{1,0:T(1,128)} %constant.2.clone.freq), custom_call_target="tpu_custom_call" | custom-call | tf_op jit(solution)/shard_map/latent_attention/pallas_call | solution.py:375
  53.6 1.7 %copy.9 = bf16[128,1024]{1,0:T(8,128)(2,1)} copy(bf16[128,1024]{1,0:T(8,128)(2,1)} %latent_attention.1) | data formatting | bytes 524288

commit v3 on v2

--- a/solution.py
+++ b/solution.py
@@ -15,10 +15,10 @@
 V_DIM = 128
 TOK = 128
 HEADS = 8
+HALF = 64
 ROWS = TOK * HEADS
 TP = 8
 SLICE = TOK // TP
-UNIT = 8 * SLICE
 EPSILON = 1e-06
 LOG2E = 1.4426950408889634
 EXP_SCALE = 192.0 ** (-0.5) * LOG2E
@@ -46,31 +46,38 @@
     return (i + (0, sign, 4 - sign, 2)[label]) % 4
 
 
+def is_masked(lineage, a, b):
+    return (b, a)[lineage] in NEAR
+
+
 def arrange():
     stages = (
         ((ME, ME),),
-        ((MATE, ME), (CROSS, ME), (FAR, ME), (ME, MATE), (ME, CROSS)),
-        ((CROSS, MATE), (FAR, MATE), (MATE, CROSS), (CROSS, CROSS)),
-        ((MATE, MATE), (FAR, CROSS)),
-        ((ME, FAR), (CROSS, FAR)),
-        ((MATE, FAR), (FAR, FAR)),
+        ((MATE, ME), (CROSS, ME), (FAR, ME)),
+        ((ME, MATE), (ME, CROSS), (ME, FAR)),
+        ((MATE, MATE), (MATE, CROSS), (MATE, FAR)),
+        ((CROSS, MATE), (CROSS, CROSS), (CROSS, FAR)),
+        ((FAR, MATE), (FAR, CROSS), (FAR, FAR)),
     )
-    labels = []
-    for masked in (True, False):
-        for stage in stages:
-            for lineage in range(2):
-                labels += [(lineage, a, b) for a, b in stage if ((b, a)[lineage] in NEAR) == masked]
-    return labels
-
-
-LABELS = arrange()
+    labels, bounds = [], []
+    for stage in stages:
+        both = [(lineage, a, b) for lineage in range(2) for a, b in stage]
+        free = [(*label, part) for label in both if not is_masked(*label) for part in range(2)]
+        masked = [(*label, part) for part in range(2) for label in both if is_masked(*label)]
+        start = len(labels)
+        labels += free + masked
+        bounds.append((start, start + len(free), start + len(free) + len(masked) // 2, len(labels)))
+    return labels, bounds
+
+
+LABELS, BOUNDS = arrange()
 PLACE = {label: place for place, label in enumerate(LABELS)}
 
 
 def kernel(
     hidden, w_down, gain, q_latent, q_rope, w_value, freq, out,
     hid_v, wd_v, ql_v, qr_v, wv_v, partial, sums, keys, q_f32, queries, cos_t, sin_t, acc, top, total,
-    load_sem, rs_s, rs_r, z_s, z_r, a_s, a_r, b_s, b_r, f_s, f_r, c_s, c_r,
+    load_sem, rs_s, rs_r, z_s, z_r, a_s, a_r, b_s, b_r, c_s, c_r,
 ):
     seq = lax.axis_index("seq")
     tp = lax.axis_index("tp")
@@ -171,18 +178,19 @@
     rope_swapped = jnp.concatenate([rope[:, ROPE // 2:], rope[:, :ROPE // 2]], 1)
     rope = rope * cos_t[mine, :ROPE] + rope_swapped * sin_t[mine, :ROPE]
 
-    def unit_at(lineage, a, b):
-        first, second = PLACE[0, a, b], PLACE[1, a, b]
+    def unit_at(lineage, a, b, part):
+        first, second = PLACE[0, a, b, part], PLACE[1, a, b, part]
         place = first + (second - first) * lineage
-        return keys.at[pl.ds(pl.multiple_of(place * UNIT, UNIT), UNIT), :]
-
-    def unit(a, b):
-        return unit_at(core, a, b)
-
-    own_place = PLACE[0, ME, ME] + (PLACE[1, ME, ME] - PLACE[0, ME, ME]) * core
+        return keys.at[pl.ds(pl.multiple_of(place * HALF, HALF), HALF), :]
+
+    def unit(a, b, part):
+        return unit_at(core, a, b, part)
+
+    own_place = [PLACE[0, ME, ME, part] + (PLACE[1, ME, ME, part] - PLACE[0, ME, ME, part]) * core for part in range(2)]
 
     def slot(z_):
-        return keys.at[pl.ds(pl.multiple_of(own_place * UNIT + z_ * SLICE, SLICE), SLICE), :]
+        place = own_place[0] + (own_place[1] - own_place[0]) * (z_ // 4)
+        return keys.at[pl.ds(pl.multiple_of(place * HALF + (z_ % 4) * SLICE, SLICE), SLICE), :]
 
     slot(z)[...] = jnp.concatenate([latent, rope], 1).astype(jnp.bfloat16)
 
@@ -203,159 +211,147 @@
             return late | jnp.logical_not(lineage_even)
         return late
 
+    full = early | (z >= 4)
+
+    def both(one, two):
+        return two if one is True else one if two is True else one & two
+
+    def kept(part, lineage_even, a, b):
+        if part == 0 or not (a in NEAR or b in NEAR):
+            return True
+        if a in NEAR and b in NEAR:
+            return full
+        return full | (jnp.logical_not(lineage_even) if b in NEAR else lineage_even)
+
     def send_a(a):
         cond = True if a == MATE else even | early
-        start(cond, unit(ME, ME), unit(a, ME), a_s.at[a], a_r.at[a], plane(near(a_me, a), b_me))
+        for part in range(2):
+            start(
+                both(cond, kept(part, even, a, ME)), unit(ME, ME, part), unit(a, ME, part),
+                a_s.at[a, part], a_r.at[a, part], plane(near(a_me, a), b_me),
+            )
 
     def send_b(a, b):
         if b == MATE:
             cond = True if a in NEAR else even | late
         else:
             cond = (even & early) | odd if a in NEAR else (even & early) | (odd & late)
-        start(cond, unit(a, ME), unit(a, b), b_s.at[b, a], b_r.at[b, a], plane(a_me, near(b_me, b)))
-
-    def forward(a):
-        came, goes = (CROSS, MATE) if a in NEAR else (MATE, CROSS)
-        if goes == MATE:
-            cond = odd | late
-        else:
-            cond = (even & early) | (odd & late)
-        start(cond, unit(a, came), unit(a, FAR), f_s.at[a], f_r.at[a], plane(a_me, near(b_me, goes)))
+        for part in range(2):
+            start(
+                both(cond, kept(part, even, a, b)), unit(a, ME, part), unit(a, b, part),
+                b_s.at[b, a, part], b_r.at[b, a, part], plane(a_me, near(b_me, b)),
+            )
 
     def to_sibling(a, b):
-        start(needed(even, a, b), unit(a, b), unit(a, b), c_s.at[b, a], c_r.at[b, a], sibling)
-
-    def arrived(cond, ref, recv_sem):
-        maybe(cond, copy(ref, ref, c_s.at[0, 0], recv_sem, sibling).wait_recv)
+        for part in range(2):
+            start(
+                both(needed(even, a, b), kept(part, even, a, b)), unit(a, b, part), unit(a, b, part),
+                c_s.at[b, a, part], c_r.at[b, a, part], sibling,
+            )
+
+    def arrived(lineage, lineage_even, a, b, recv_sem):
+        for part in range(2):
+            ref = unit_at(lineage, a, b, part)
+            one = copy(ref, ref, c_s.at[0, 0, 0], recv_sem.at[part], sibling)
+            maybe(both(needed(lineage_even, a, b), kept(part, lineage_even, a, b)), one.wait_recv)
 
     def got_a(a):
-        arrived(needed(even, a, ME), unit(a, ME), a_r.at[a])
+        arrived(core, even, a, ME, a_r.at[a])
 
     def got_b(a, b):
-        arrived(needed(even, a, b), unit(a, b), b_r.at[b, a])
-
-    def got_far(a):
-        arrived(needed(even, a, FAR), unit(a, FAR), f_r.at[a])
+        arrived(core, even, a, b, b_r.at[b, a])
 
     def got_sibling(*labels):
         for a, b in labels:
-            arrived(needed(odd, a, b), unit_at(1 - core, a, b), c_r.at[b, a])
-
-    row = lax.broadcasted_iota(jnp.int32, (UNIT, TOK), 0)
-    token = lax.broadcasted_iota(jnp.int32, (UNIT, TOK), 1)
+            arrived(1 - core, odd, a, b, c_r.at[b, a])
+
+    row = lax.broadcasted_iota(jnp.int32, (HALF, TOK), 0)
+    token = lax.broadcasted_iota(jnp.int32, (HALF, TOK), 1)
     ahead = (row // SLICE) * (2 * TOK) + row % SLICE - token
 
     def bias(place):
-        lineage, a, b = LABELS[place]
+        lineage, a, b, part = LABELS[place]
         x_label, y_label = (a, b) if lineage == 0 else (b, a)
-        base = (lineage - core - 2 * z) * TOK + (near(x, x_label) * 2 + near(y, y_label) % 2) * SLICE
-        return jnp.concatenate([jnp.where(ahead + base <= 0, 0.0, -1e30)] * HEADS, 1)
-
-    def attend(masked, free, first=False):
-        rows, scores = [], []
-        for (begin, end), is_masked in ((masked, True), (free, False)):
-            if begin == end:
-                continue
-            rows.append(keys[begin * UNIT:end * UNIT, :])
-            block = dot(rows[-1], queries[...], NT)
-            if is_masked:
-                block = block + jnp.concatenate([bias(place) for place in range(begin, end)], 0)
-            scores.append(block)
-        new_top = functools.reduce(jnp.maximum, [jnp.max(block, 0, keepdims=True) for block in scores])
+        base = (lineage - core - 2 * z + 8 * part) * TOK + (near(x, x_label) * 2 + near(y, y_label) % 2) * SLICE
+        return jnp.concatenate([jnp.where(ahead + base <= 0, 0.0, -1e30)] * (HEADS // 2), 1)
+
+    def attend(half, begin, end, first=False):
+        cut = slice(half * ROWS // 2, (half + 1) * ROWS // 2)
+        rows = keys[begin * HALF:end * HALF, :]
+        scores = dot(rows, queries[cut, :], NT)
+        masked = [place for place in range(begin, end) if is_masked(*LABELS[place][:3])]
+        if masked:
+            low, high = (masked[0] - begin) * HALF, (masked[-1] + 1 - begin) * HALF
+            blocks = [scores[low:high] + jnp.concatenate([bias(place) for place in masked], 0)]
+            if low > 0:
+                blocks.insert(0, scores[:low])
+            if high < scores.shape[0]:
+                blocks.append(scores[high:])
+            scores = jnp.concatenate(blocks, 0)
+        new_top = jnp.max(scores, 0, keepdims=True)
         if not first:
-            new_top = jnp.maximum(top[0:1, :], new_top)
+            new_top = jnp.maximum(top[0:1, cut], new_top)
         shift = new_top * EXP_SCALE
-        added, mixed = 0.0, 0.0
-        for keys_here, block in zip(rows, scores):
-            weights = jnp.exp2(block * EXP_SCALE - shift)
-            added = added + jnp.sum(weights, 0, keepdims=True)
-            mixed = mixed + dot(keys_here[:, :KV_RANK], weights.astype(jnp.bfloat16), TN)
+        weights = jnp.exp2(scores * EXP_SCALE - shift)
+        added = jnp.sum(weights, 0, keepdims=True)
+        mixed = dot(rows[:, :KV_RANK], weights.astype(jnp.bfloat16), TN)
         if first:
-            total[0:1, :] = added
-            acc[...] = mixed
+            total[0:1, cut] = added
+            acc[:, cut] = mixed
         else:
-            scale = jnp.exp2(top[0:1, :] * EXP_SCALE - shift)
-            total[0:1, :] = total[0:1, :] * scale + added
-            acc[...] = acc[...] * scale + mixed
-        top[0:1, :] = new_top
-
-    def chunk(masked_late, free_late, masked_early):
-        @pl.when(late)
-        def _():
-            attend(masked_late, free_late)
-
-        if masked_early is not None:
+            scale = jnp.exp2(top[0:1, cut] * EXP_SCALE - shift)
+            total[0:1, cut] = total[0:1, cut] * scale + added
+            acc[:, cut] = acc[:, cut] * scale + mixed
+        top[0:1, cut] = new_top
+
+    def chunk(half, stage):
+        begin, masked_begin, masked_half, end = BOUNDS[stage]
+        first = stage == 0
+        if first:
+            @pl.when(full)
+            def _():
+                attend(half, begin, end, first)
+        else:
             @pl.when(early)
             def _():
-                attend(masked_early, (0, 0))
-
-    for a in (MATE, CROSS, FAR):
+                attend(half, masked_begin, end)
+
+            @pl.when(late & full)
+            def _():
+                attend(half, begin, end)
+
+        @pl.when(jnp.logical_not(full))
+        def _():
+            attend(half, begin, masked_half, first)
+
+    away = (MATE, CROSS, FAR)
+    for a in away:
         send_a(a)
-    send_b(ME, MATE)
-    send_b(ME, CROSS)
     to_sibling(ME, ME)
     got_sibling((ME, ME))
-    attend((0, 2), (0, 0), first=True)
-
-    got_a(MATE)
-    send_b(MATE, CROSS)
-    got_a(CROSS)
-    send_b(CROSS, MATE)
-    send_b(CROSS, CROSS)
-    got_a(FAR)
-    send_b(FAR, MATE)
-    send_b(FAR, CROSS)
-    send_b(MATE, MATE)
-    for a in (MATE, CROSS, FAR):
+    chunk(0, 0)
+    for b in away:
+        send_b(ME, b)
+    chunk(1, 0)
+
+    for a in away:
+        got_a(a)
+        for b in away:
+            send_b(a, b)
         to_sibling(a, ME)
-    got_b(ME, CROSS)
-    forward(ME)
-    to_sibling(ME, CROSS)
-    got_b(ME, MATE)
-    to_sibling(ME, MATE)
-    got_sibling((MATE, ME), (CROSS, ME), (FAR, ME), (ME, CROSS), (ME, MATE))
-    chunk((2, 9), (16, 19), (2, 9))
-
-    got_b(CROSS, MATE)
-    forward(CROSS)
-    to_sibling(CROSS, MATE)
-    got_b(MATE, CROSS)
-    forward(MATE)
-    to_sibling(MATE, CROSS)
-    got_b(FAR, MATE)
-    forward(FAR)
-    to_sibling(FAR, MATE)
-    got_b(CROSS, CROSS)
-    to_sibling(CROSS, CROSS)
-    got_sibling((CROSS, MATE), (MATE, CROSS), (FAR, MATE), (CROSS, CROSS))
-    chunk((9, 12), (19, 24), None)
-
-    got_b(MATE, MATE)
-    to_sibling(MATE, MATE)
-    got_b(FAR, CROSS)
-    to_sibling(FAR, CROSS)
-    got_sibling((MATE, MATE), (FAR, CROSS))
-
-    @pl.when(early)
-    def _():
-        attend((9, 14), (0, 0))
-
-    got_far(ME)
-    to_sibling(ME, FAR)
-    got_far(CROSS)
-    to_sibling(CROSS, FAR)
-    got_sibling((ME, FAR), (CROSS, FAR))
-    chunk((12, 15), (24, 29), None)
-
-    got_far(MATE)
-    to_sibling(MATE, FAR)
-    got_far(FAR)
-    to_sibling(FAR, FAR)
-    got_sibling((MATE, FAR), (FAR, FAR))
-    chunk((15, 16), (29, 32), (14, 16))
+    got_sibling(*((a, ME) for a in away))
+    for stage, a in enumerate((ME, *away), 1):
+        chunk(0, stage)
+        for b in away:
+            got_b(a, b)
+            to_sibling(a, b)
+        chunk(1, stage)
+        got_sibling(*((a, b) for b in away))
+    chunk(0, 5)
+    chunk(1, 5)
 
     loads[4].wait()
-    mixed = (acc[...] / total[0:1, :]).astype(jnp.bfloat16)
+    mixed = (acc[...] * (1.0 / total[0:1, :])).astype(jnp.bfloat16)
     for h in range(HEADS):
         cut = slice(h * TOK, (h + 1) * TOK)
         out[:, h * V_DIM:(h + 1) * V_DIM] = dot(mixed[:, cut], wv_v[h], TN).astype(jnp.bfloat16)
@@ -386,7 +382,7 @@
             pltpu.VMEM((HEADS, KV_RANK, V_DIM), bf16),
             pltpu.VMEM((TOK, WIDTH), f32),
             pltpu.VMEM((TP, SLICE, WIDTH), f32),
-            pltpu.VMEM((32 * UNIT, WIDTH), bf16),
+            pltpu.VMEM((64 * HALF, WIDTH), bf16),
             pltpu.VMEM((KV_RANK // 128, ROWS, 128), f32),
             pltpu.VMEM((ROWS, WIDTH), bf16),
             pltpu.VMEM((TOK, 128), f32),
@@ -397,10 +393,9 @@
             dma((5,)),
             dma((8,)), dma((8,)),
             dma((8,)), dma((8,)),
-            dma((4,)), dma((4,)),
-            dma((4, 4)), dma((4, 4)),
-            dma((4,)), dma((4,)),
-            dma((4, 4)), dma((4, 4)),
+            dma((4, 2)), dma((4, 2)),
+            dma((4, 4, 2)), dma((4, 4, 2)),
+            dma((4, 4, 2)), dma((4, 4, 2)),
         ],
         compiler_params=pltpu.CompilerParams(
             collective_id=0, has_side_effects=True, vmem_limit_bytes=60 * 2**20

time: 55.4 us -> 47.4 us (0.86)
  Pallas kernels: 53.6 us -> 45 us
    pallas_call x1, Pallas kernels: 53.6 us -> 45 us  [shards(): pl.pallas_call(kernel, name='latent_attention', out_shape=jax.ShapeDtypeS...]
where the time goes in v3:
time: 47.4 us; the launch traced here: 46.7 us
  Pallas kernels  45 us (95%)
  local copies, waits for them, and re-layouts  1.67 us (4%)
    pallas_call x1, Pallas kernels, shards(): pl.pallas_call(kernel, name='latent_attention', out_shape=jax.ShapeDtypeS...  45 us
    unnamed x1, local copies, waits for them, and re-layouts  1.67 us

profile of v3, /device:TPU:27, one launch (start us, length us, event | category | flops | bytes accessed | tf_op | source)
XLA Modules:
  0.0 46.7 jit_solution(11636444183818305930)
XLA Ops:
  0.0 45.0 %latent_attention.1 = bf16[128,1024]{1,0:T(8,128)(2,1)} custom-call(bf16[128,896]{1,0:T(8,128)(2,1)} %hidden.1, bf16[576,896]{1,0:T(8,128)(2,1)} %bitcast.4, f32[1,512]{1,0:T(1,128)} %bitcast.5, bf16[1024,512]{1,0:T(8,128)(2,1)} %bitcast.3, bf16[128,512]{1,0:T(8,128)(2,1)} %q_rope.1, bf16[8,512,128]{2,1,0:T(8,128)(2,1)} %w_value.1, f32[1,128]{1,0:T(1,128)} %constant.2.clone.freq), custom_call_target="tpu_custom_call" | custom-call | tf_op jit(solution)/shard_map/latent_attention/pallas_call | solution.py:371
  45.0 1.7 %copy.9 = bf16[128,1024]{1,0:T(8,128)(2,1)} copy(bf16[128,1024]{1,0:T(8,128)(2,1)} %latent_attention.1) | data formatting | bytes 524288

commit v4 on v3

--- a/solution.py
+++ b/solution.py
@@ -76,7 +76,7 @@
 
 def kernel(
     hidden, w_down, gain, q_latent, q_rope, w_value, freq, out,
-    hid_v, wd_v, ql_v, qr_v, wv_v, partial, sums, keys, q_f32, queries, cos_t, sin_t, acc, top, total,
+    hid_v, wd_v, ql_v, qr_v, wv_v, partial, sums, pieces, keys, q_f32, queries, cos_t, sin_t, acc, top, total,
     load_sem, rs_s, rs_r, z_s, z_r, a_s, a_r, b_s, b_r, c_s, c_r,
 ):
     seq = lax.axis_index("seq")
@@ -163,7 +163,8 @@
             queries[h * TOK:(h + 1) * TOK, c * 128:(c + 1) * 128] = q_f32[
                 c, pl.ds(h, TOK, stride=HEADS), :
             ].astype(jnp.bfloat16)
-        queries[h * TOK:(h + 1) * TOK, KV_RANK:] = rotated[:, h * ROPE:(h + 1) * ROPE]
+        mine = rotated[:, h * ROPE:(h + 1) * ROPE]
+        queries[h * TOK:(h + 1) * TOK, KV_RANK:] = jnp.concatenate([mine, mine], 1)
 
     for d in range(1, TP):
         copy(rows_of(tp), sums.at[d], rs_s.at[d], rs_r.at[d], (seq, tp)).wait_recv()
@@ -181,7 +182,7 @@
     def unit_at(lineage, a, b, part):
         first, second = PLACE[0, a, b, part], PLACE[1, a, b, part]
         place = first + (second - first) * lineage
-        return keys.at[pl.ds(pl.multiple_of(place * HALF, HALF), HALF), :]
+        return keys.at[place]
 
     def unit(a, b, part):
         return unit_at(core, a, b, part)
@@ -189,8 +190,7 @@
     own_place = [PLACE[0, ME, ME, part] + (PLACE[1, ME, ME, part] - PLACE[0, ME, ME, part]) * core for part in range(2)]
 
     def slot(z_):
-        place = own_place[0] + (own_place[1] - own_place[0]) * (z_ // 4)
-        return keys.at[pl.ds(pl.multiple_of(place * HALF + (z_ % 4) * SLICE, SLICE), SLICE), :]
+        return pieces.at[z_]
 
     slot(z)[...] = jnp.concatenate([latent, rope], 1).astype(jnp.bfloat16)
 
@@ -199,6 +199,14 @@
     for d in range(1, 8):
         there = slot((z - d) % 8)
         copy(there, there, z_s.at[d], z_r.at[d], sibling).wait_recv()
+    for part in range(2):
+        four = [pieces[part * 4 + i] for i in range(4)]
+        for i in range(4):
+            for c in range(KV_RANK // 128):
+                keys[own_place[part], c * HALF + i * SLICE:c * HALF + (i + 1) * SLICE, :] = four[i][:, c * 128:(c + 1) * 128]
+        for i in range(2):
+            at = KV_RANK // 128 * HALF + i * SLICE
+            keys[own_place[part], at:at + SLICE, :] = jnp.concatenate([four[i][:, KV_RANK:], four[i + 2][:, KV_RANK:]], 1)
 
     early, late, even, odd = y_hi == 0, y_hi == 1, core == 0, core == 1
 
@@ -275,26 +283,37 @@
         base = (lineage - core - 2 * z + 8 * part) * TOK + (near(x, x_label) * 2 + near(y, y_label) % 2) * SLICE
         return jnp.concatenate([jnp.where(ahead + base <= 0, 0.0, -1e30)] * (HEADS // 2), 1)
 
+    sides = [(lane < ROPE).astype(jnp.bfloat16), (lane >= ROPE).astype(jnp.bfloat16)]
+
     def attend(half, begin, end, first=False):
         cut = slice(half * ROWS // 2, (half + 1) * ROWS // 2)
-        rows = keys[begin * HALF:end * HALF, :]
-        scores = dot(rows, queries[cut, :], NT)
+        blocks = range(begin, end)
+        rows = jnp.concatenate(
+            [
+                jnp.concatenate([keys[place, c * HALF:(c + 1) * HALF, :] for place in blocks], 0)
+                for c in range(KV_RANK // 128)
+            ],
+            1,
+        )
+        pairs = [keys[place, KV_RANK // 128 * HALF:, :] for place in blocks]
+        ropes = jnp.concatenate([side * pair for pair in pairs for side in sides], 0)
+        scores = dot(jnp.concatenate([rows, ropes], 1), queries[cut, :], NT)
         masked = [place for place in range(begin, end) if is_masked(*LABELS[place][:3])]
         if masked:
             low, high = (masked[0] - begin) * HALF, (masked[-1] + 1 - begin) * HALF
-            blocks = [scores[low:high] + jnp.concatenate([bias(place) for place in masked], 0)]
+            split = [scores[low:high] + jnp.concatenate([bias(place) for place in masked], 0)]
             if low > 0:
-                blocks.insert(0, scores[:low])
+                split.insert(0, scores[:low])
             if high < scores.shape[0]:
-                blocks.append(scores[high:])
-            scores = jnp.concatenate(blocks, 0)
+                split.append(scores[high:])
+            scores = jnp.concatenate(split, 0)
         new_top = jnp.max(scores, 0, keepdims=True)
         if not first:
             new_top = jnp.maximum(top[0:1, cut], new_top)
         shift = new_top * EXP_SCALE
         weights = jnp.exp2(scores * EXP_SCALE - shift)
         added = jnp.sum(weights, 0, keepdims=True)
-        mixed = dot(rows[:, :KV_RANK], weights.astype(jnp.bfloat16), TN)
+        mixed = dot(rows, weights.astype(jnp.bfloat16), TN)
         if first:
             total[0:1, cut] = added
             acc[:, cut] = mixed
@@ -308,21 +327,11 @@
         begin, masked_begin, masked_half, end = BOUNDS[stage]
         first = stage == 0
         if first:
-            @pl.when(full)
-            def _():
-                attend(half, begin, end, first)
+            pl.when(full)(lambda: attend(half, begin, end, first))
         else:
-            @pl.when(early)
-            def _():
-                attend(half, masked_begin, end)
-
-            @pl.when(late & full)
-            def _():
-                attend(half, begin, end)
-
-        @pl.when(jnp.logical_not(full))
-        def _():
-            attend(half, begin, masked_half, first)
+            pl.when(early)(lambda: attend(half, masked_begin, end))
+            pl.when(late & full)(lambda: attend(half, begin, end))
+        pl.when(jnp.logical_not(full))(lambda: attend(half, begin, masked_half, first))
 
     away = (MATE, CROSS, FAR)
     for a in away:
@@ -382,9 +391,10 @@
             pltpu.VMEM((HEADS, KV_RANK, V_DIM), bf16),
             pltpu.VMEM((TOK, WIDTH), f32),
             pltpu.VMEM((TP, SLICE, WIDTH), f32),
-            pltpu.VMEM((64 * HALF, WIDTH), bf16),
+            pltpu.VMEM((8, SLICE, WIDTH), bf16),
+            pltpu.VMEM((64, HALF // 2 * 9, 128), bf16),
             pltpu.VMEM((KV_RANK // 128, ROWS, 128), f32),
-            pltpu.VMEM((ROWS, WIDTH), bf16),
+            pltpu.VMEM((ROWS, WIDTH + ROPE), bf16),
             pltpu.VMEM((TOK, 128), f32),
             pltpu.VMEM((TOK, 128), f32),
             pltpu.VMEM((KV_RANK, ROWS), f32),

time: 47.4 us -> 46.6 us (0.983)
  the two profiles are of different devices: /device:TPU:27 before, /device:TPU:25 now
where the time goes in v4:
time: 46.6 us; the launch traced here: 46.5 us
  Pallas kernels  44.8 us (96%)
  local copies, waits for them, and re-layouts  1.67 us (4%)
    pallas_call x1, Pallas kernels, shards(): pl.pallas_call(kernel, name='latent_attention', out_shape=jax.ShapeDtypeS...  44.8 us
    unnamed x1, local copies, waits for them, and re-layouts  1.67 us

profile of v4, /device:TPU:25, one launch (start us, length us, event | category | flops | bytes accessed | tf_op | source)
XLA Modules:
  0.0 46.5 jit_solution(12488226494638825033)
XLA Ops:
  0.0 44.8 %latent_attention.1 = bf16[128,1024]{1,0:T(8,128)(2,1)} custom-call(bf16[128,896]{1,0:T(8,128)(2,1)} %hidden.1, bf16[576,896]{1,0:T(8,128)(2,1)} %bitcast.4, f32[1,512]{1,0:T(1,128)} %bitcast.5, bf16[1024,512]{1,0:T(8,128)(2,1)} %bitcast.3, bf16[128,512]{1,0:T(8,128)(2,1)} %q_rope.1, bf16[8,512,128]{2,1,0:T(8,128)(2,1)} %w_value.1, f32[1,128]{1,0:T(1,128)} %constant.2.clone.freq), custom_call_target="tpu_custom_call" | custom-call | tf_op jit(solution)/shard_map/latent_attention/pallas_call | solution.py:380
  44.8 1.7 %copy.9 = bf16[128,1024]{1,0:T(8,128)(2,1)} copy(bf16[128,1024]{1,0:T(8,128)(2,1)} %latent_attention.1) | data formatting | bytes 524288

commit v5 on v4

--- a/solution.py
+++ b/solution.py
@@ -62,7 +62,7 @@
     labels, bounds = [], []
     for stage in stages:
         both = [(lineage, a, b) for lineage in range(2) for a, b in stage]
-        free = [(*label, part) for label in both if not is_masked(*label) for part in range(2)]
+        free = [(*label, part) for label in both[::-1] if not is_masked(*label) for part in range(2)]
         masked = [(*label, part) for part in range(2) for label in both if is_masked(*label)]
         start = len(labels)
         labels += free + masked
@@ -285,8 +285,7 @@
 
     sides = [(lane < ROPE).astype(jnp.bfloat16), (lane >= ROPE).astype(jnp.bfloat16)]
 
-    def attend(half, begin, end, first=False):
-        cut = slice(half * ROWS // 2, (half + 1) * ROWS // 2)
+    def attend(halves, begin, end, first=False):
         blocks = range(begin, end)
         rows = jnp.concatenate(
             [
@@ -297,67 +296,109 @@
         )
         pairs = [keys[place, KV_RANK // 128 * HALF:, :] for place in blocks]
         ropes = jnp.concatenate([side * pair for pair in pairs for side in sides], 0)
-        scores = dot(jnp.concatenate([rows, ropes], 1), queries[cut, :], NT)
-        masked = [place for place in range(begin, end) if is_masked(*LABELS[place][:3])]
-        if masked:
-            low, high = (masked[0] - begin) * HALF, (masked[-1] + 1 - begin) * HALF
-            split = [scores[low:high] + jnp.concatenate([bias(place) for place in masked], 0)]
-            if low > 0:
-                split.insert(0, scores[:low])
-            if high < scores.shape[0]:
-                split.append(scores[high:])
-            scores = jnp.concatenate(split, 0)
-        new_top = jnp.max(scores, 0, keepdims=True)
-        if not first:
-            new_top = jnp.maximum(top[0:1, cut], new_top)
-        shift = new_top * EXP_SCALE
-        weights = jnp.exp2(scores * EXP_SCALE - shift)
-        added = jnp.sum(weights, 0, keepdims=True)
-        mixed = dot(rows, weights.astype(jnp.bfloat16), TN)
-        if first:
-            total[0:1, cut] = added
-            acc[:, cut] = mixed
-        else:
-            scale = jnp.exp2(top[0:1, cut] * EXP_SCALE - shift)
-            total[0:1, cut] = total[0:1, cut] * scale + added
-            acc[:, cut] = acc[:, cut] * scale + mixed
-        top[0:1, cut] = new_top
-
-    def chunk(half, stage):
+        wide_rows = jnp.concatenate([rows, ropes], 1)
+        masked = [place for place in blocks if is_masked(*LABELS[place][:3])]
+        low = (masked[0] - begin) * HALF if masked else 0
+        high = (masked[-1] + 1 - begin) * HALF if masked else 0
+        mask = jnp.concatenate([bias(place) for place in masked], 0) if masked else None
+        cuts = [slice(half * ROWS // 2, (half + 1) * ROWS // 2) for half in halves]
+
+        def scores_of(cut):
+            scores = dot(wide_rows, queries[cut, :], NT)
+            if masked:
+                split = [scores[low:high] + mask]
+                if low > 0:
+                    split.insert(0, scores[:low])
+                if high < scores.shape[0]:
+                    split.append(scores[high:])
+                scores = jnp.concatenate(split, 0)
+            return scores
+
+        def weights_of(cut, scores):
+            new_top = jnp.max(scores, 0, keepdims=True)
+            scale = None
+            if not first:
+                new_top = jnp.maximum(top[0:1, cut], new_top)
+            shift = new_top * EXP_SCALE
+            weights = jnp.exp2(scores * EXP_SCALE - shift)
+            added = jnp.sum(weights, 0, keepdims=True)
+            if first:
+                total[0:1, cut] = added
+            else:
+                scale = jnp.exp2(top[0:1, cut] * EXP_SCALE - shift)
+                total[0:1, cut] = total[0:1, cut] * scale + added
+            top[0:1, cut] = new_top
+            return weights.astype(jnp.bfloat16), scale
+
+        all_scores = [scores_of(cut) for cut in cuts]
+        all_weights = [weights_of(cut, scores) for cut, scores in zip(cuts, all_scores)]
+        for cut, (weights, scale) in zip(cuts, all_weights):
+            mixed = dot(rows, weights, TN)
+            acc[:, cut] = mixed if first else acc[:, cut] * scale + mixed
+
+    def chunk(stage, halves=(0, 1)):
         begin, masked_begin, masked_half, end = BOUNDS[stage]
         first = stage == 0
         if first:
-            pl.when(full)(lambda: attend(half, begin, end, first))
+            pl.when(full)(lambda: attend(halves, begin, end, first))
         else:
-            pl.when(early)(lambda: attend(half, masked_begin, end))
-            pl.when(late & full)(lambda: attend(half, begin, end))
-        pl.when(jnp.logical_not(full))(lambda: attend(half, begin, masked_half, first))
+            pl.when(early)(lambda: attend(halves, masked_begin, end))
+            pl.when(late & full)(lambda: attend(halves, begin, end))
+        pl.when(jnp.logical_not(full))(lambda: attend(halves, begin, masked_half, first))
 
     away = (MATE, CROSS, FAR)
-    for a in away:
+
+    def landed(a):
+        for b in away:
+            got_b(a, b)
+            to_sibling(a, b)
+
+    def shared(a):
+        got_sibling(*((a, b) for b in away))
+
+    order = (MATE, CROSS, FAR)
+    for a in order:
         send_a(a)
     to_sibling(ME, ME)
     got_sibling((ME, ME))
-    chunk(0, 0)
-    for b in away:
+    for b in order:
         send_b(ME, b)
-    chunk(1, 0)
-
+    chunk(0)
     for a in away:
         got_a(a)
-        for b in away:
+        for b in order:
             send_b(a, b)
         to_sibling(a, ME)
     got_sibling(*((a, ME) for a in away))
-    for stage, a in enumerate((ME, *away), 1):
-        chunk(0, stage)
-        for b in away:
-            got_b(a, b)
-            to_sibling(a, b)
-        chunk(1, stage)
-        got_sibling(*((a, b) for b in away))
-    chunk(0, 5)
-    chunk(1, 5)
+    landed(ME)
+    chunk(1)
+    shared(ME)
+    landed(MATE)
+    chunk(2)
+    shared(MATE)
+    chunk(3, (0,))
+    landed(CROSS)
+    chunk(3, (1,))
+    shared(CROSS)
+    chunk(4)
+    landed(FAR)
+    begin, masked_begin, masked_half, last = BOUNDS[5]
+    middle = begin + 6
+
+    def even_lineage():
+        pl.when(early)(lambda: attend((0, 1), masked_begin, last))
+        pl.when(late & full)(lambda: attend((0, 1), middle, last))
+        pl.when(jnp.logical_not(full))(lambda: attend((0, 1), middle, masked_half))
+
+    def odd_lineage():
+        pl.when(late)(lambda: attend((0, 1), begin, middle))
+
+    pl.when(even)(even_lineage)
+    pl.when(odd)(odd_lineage)
+    shared(FAR)
+    pl.when(even)(odd_lineage)
+    pl.when(odd)(even_lineage)
+
 
     loads[4].wait()
     mixed = (acc[...] * (1.0 / total[0:1, :])).astype(jnp.bfloat16)

time: 46.6 us -> 46.7 us (level)
  the two profiles are of different devices: /device:TPU:25 before, /device:TPU:27 now
where the time goes in v5:
time: 46.7 us; the launch traced here: 46 us
  Pallas kernels  44.3 us (95%)
  local copies, waits for them, and re-layouts  1.67 us (4%)
    pallas_call x1, Pallas kernels, shards(): pl.pallas_call(kernel, name='latent_attention', out_shape=jax.ShapeDtypeS...  44.3 us
    unnamed x1, local copies, waits for them, and re-layouts  1.67 us

profile of v5, /device:TPU:27, one launch (start us, length us, event | category | flops | bytes accessed | tf_op | source)
XLA Modules:
  0.0 46.0 jit_solution(16054763507124981555)
XLA Ops:
  0.0 44.3 %latent_attention.1 = bf16[128,1024]{1,0:T(8,128)(2,1)} custom-call(bf16[128,896]{1,0:T(8,128)(2,1)} %hidden.1, bf16[576,896]{1,0:T(8,128)(2,1)} %bitcast.4, f32[1,512]{1,0:T(1,128)} %bitcast.5, bf16[1024,512]{1,0:T(8,128)(2,1)} %bitcast.3, bf16[128,512]{1,0:T(8,128)(2,1)} %q_rope.1, bf16[8,512,128]{2,1,0:T(8,128)(2,1)} %w_value.1, f32[1,128]{1,0:T(1,128)} %constant.2.clone.freq), custom_call_target="tpu_custom_call" | custom-call | tf_op jit(solution)/shard_map/latent_attention/pallas_call | solution.py:421
  44.3 1.7 %copy.9 = bf16[128,1024]{1,0:T(8,128)(2,1)} copy(bf16[128,1024]{1,0:T(8,128)(2,1)} %latent_attention.1) | data formatting | bytes 524288

commit v6 on v5

--- a/solution.py
+++ b/solution.py
@@ -404,7 +404,7 @@
     mixed = (acc[...] * (1.0 / total[0:1, :])).astype(jnp.bfloat16)
     for h in range(HEADS):
         cut = slice(h * TOK, (h + 1) * TOK)
-        out[:, h * V_DIM:(h + 1) * V_DIM] = dot(mixed[:, cut], wv_v[h], TN).astype(jnp.bfloat16)
+        out[:, h * V_DIM:(h + 1) * V_DIM] = dot(mixed[:, cut], wv_v[h], TN)
     for cond, one in sent:
         maybe(cond, one.wait_send)
 
@@ -418,10 +418,10 @@
     bf16, f32 = jnp.bfloat16, jnp.float32
     dma = pltpu.SemaphoreType.DMA
     width = hidden.shape[1]
-    return pl.pallas_call(
+    attended = pl.pallas_call(
         kernel,
         name="latent_attention",
-        out_shape=jax.ShapeDtypeStruct((TOK, HEADS * V_DIM), bf16),
+        out_shape=jax.ShapeDtypeStruct((TOK, HEADS * V_DIM), f32),
         in_specs=[hbm, hbm, vmem, hbm, hbm, hbm, vmem],
         out_specs=vmem,
         scratch_shapes=[
@@ -460,6 +460,7 @@
         w_value,
         freq,
     )
+    return attended.astype(bf16)
 
 
 def solution(mesh):

time: 46.7 us -> 46.9 us (level)
  other arithmetic: 0 us -> 1.78 us
  local copies, waits for them, and re-layouts: 1.67 us -> 0 us
    convert_element_type x0 -> x1, other arithmetic: none -> 1.78 us  [shards(): return attended.astype(bf16)]
    unnamed x1 -> x0, local copies, waits for them, and re-layouts: 1.67 us -> none
where the time goes in v6:
time: 46.9 us; the launch traced here: 46.2 us
  Pallas kernels  44.4 us (95%)
  other arithmetic  1.78 us (4%)
    pallas_call x1, Pallas kernels, shards(): pl.pallas_call(kernel, name='latent_attention', out_shape=jax.ShapeDtypeS...  44.4 us
    convert_element_type x1, other arithmetic, shards(): return attended.astype(bf16)  1.78 us

profile of v6, /device:TPU:27, one launch (start us, length us, event | category | flops | bytes accessed | tf_op | source)
XLA Modules:
  0.0 46.2 jit_solution(5619010732084743426)
XLA Ops:
  0.0 44.4 %latent_attention.1 = f32[128,1024]{1,0:T(8,128)} custom-call(bf16[128,896]{1,0:T(8,128)(2,1)} %hidden.1, bf16[576,896]{1,0:T(8,128)(2,1)} %bitcast.4, f32[1,512]{1,0:T(1,128)} %bitcast.5, bf16[1024,512]{1,0:T(8,128)(2,1)} %bitcast.3, bf16[128,512]{1,0:T(8,128)(2,1)} %q_rope.1, bf16[8,512,128]{2,1,0:T(8,128)(2,1)} %w_value.1, f32[1,128]{1,0:T(1,128)} %constant.2.clone.freq), custom_call_target="tpu_custom_call" | custom-call | tf_op jit(solution)/shard_map/latent_attention/pallas_call | solution.py:421
  44.4 1.8 %convert_element_type.3 = bf16[128,1024]{1,0:T(8,128)(2,1)} convert(f32[128,1024]{1,0:T(8,128)} %latent_attention.1) | non-fusion elementwise | flops 131072 | bytes 786432 | tf_op jit(solution)/shard_map/convert_element_type | solution.py:463
